TPU v7x, 256 devices: a whole 4x4x8 slice. The times are simulated.
256 devices in a mesh: ctx: 16 (over z, y_lo), head: 8 (over x, y_hi), dp: 2 (over core).
Axes of the slice: x: 4, y: 4 (y_hi: 2, y_lo: 2; y = y_hi * 2 + y_lo), z: 8, core: 2. Of those that a mesh axis runs over, the one named last changes fastest.
Arguments:
- queries: bfloat16 [24576, 5120], P(('dp', 'ctx'), 'head'), parts along dimension 0, may hold values from -60 to 60
- query_tangent: bfloat16 [24576, 5120], P(('dp', 'ctx'), 'head'), parts along dimension 0, may hold values from -6 to 6
- keys: bfloat16 [4096, 5120], P(('dp', 'ctx'), 'head'), parts along dimension 0, may hold values from -60 to 60
- key_tangent: bfloat16 [4096, 5120], P(('dp', 'ctx'), 'head'), parts along dimension 0, may hold values from -6 to 6
- values: bfloat16 [4096, 5120], P(('dp', 'ctx'), 'head'), parts along dimension 0, may hold values from -6 to 6
- value_tangent: bfloat16 [4096, 5120], P(('dp', 'ctx'), 'head'), parts along dimension 0, may hold values from -6 to 6
- query_gain: float32 [5120], P('head'), may hold values from 0.8 to 2.5
- key_gain: float32 [5120], P('head'), may hold values from 0.8 to 2.5
Outputs:
- attended: bfloat16 [24576, 5120], P(('dp', 'ctx'), 'head'), parts along dimension 0
- attended_tangent: bfloat16 [24576, 5120], P(('dp', 'ctx'), 'head'), parts along dimension 0
There are 2 independent parts, one for each index of `dp`. A program takes and returns all parts, laid end to end along the dimension named above; an argument that names none is the same for every part. Nothing has to cross between parts.
All inputs are finite; a program needn't handle non-finite values.
Results may differ from a plain program's by a relative error of at most 0.012.
The roundings to bfloat16 on the way count: a program that leaves them out, or rounds other values in their place, can miss the bound.
Values may be sent and summed in bfloat16 or wider, within the bound.
A program may use at most 128 MiB of HBM per device.

v0:
```python
import jax
import jax.numpy as jnp
from jax import lax
from jax.sharding import PartitionSpec as P

HEAD_DIM = 128


def finish(field, tangent, sum_sq, sum_cross, total_width, gain):
    mean_sq = (sum_sq / total_width)[:, None]
    mean_cross = (sum_cross / total_width)[:, None]
    inverse = lax.rsqrt(mean_sq + 1e-06)
    normed = (field * inverse * gain).astype(jnp.bfloat16)
    normed_tangent = (gain * (tangent * inverse - field * inverse**3 * mean_cross)).astype(
        jnp.bfloat16
    )
    return (normed, normed_tangent)


def by_heads(field, heads):
    return field.reshape(field.shape[0], heads, HEAD_DIM).transpose(1, 0, 2)


def head_update(items):
    (
        q_head,
        dq_head,
        k_head,
        dk_head,
        v_head,
        dv_head,
        running,
        total,
        spread,
        primal_sum,
        tangent_sum,
    ) = items
    scale = HEAD_DIM ** (-0.5)
    scores = jnp.einsum("qd,kd->qk", q_head, k_head, preferred_element_type=jnp.float32) * scale
    score_tangent = (
        jnp.einsum("qd,kd->qk", dq_head, k_head, preferred_element_type=jnp.float32)
        + jnp.einsum("qd,kd->qk", q_head, dk_head, preferred_element_type=jnp.float32)
    ) * scale
    newest = jnp.maximum(running, jnp.max(scores, axis=1))
    factor = jnp.exp(running - newest)
    weights = jnp.exp(scores - newest[:, None])
    mixed = weights * score_tangent
    total = factor * total + jnp.sum(weights, axis=1)
    spread = factor * spread + jnp.sum(mixed, axis=1)
    weights_low = weights.astype(jnp.bfloat16)
    mixed_low = mixed.astype(jnp.bfloat16)
    primal_sum = factor[:, None] * primal_sum + jnp.dot(
        weights_low, v_head, preferred_element_type=jnp.float32
    )
    tangent_sum = (
        factor[:, None] * tangent_sum
        + jnp.dot(mixed_low, v_head, preferred_element_type=jnp.float32)
        + jnp.dot(weights_low, dv_head, preferred_element_type=jnp.float32)
    )
    return (newest, total, spread, primal_sum, tangent_sum)


def shards(queries, query_tangent, keys, key_tangent, values, value_tangent, query_gain, key_gain):
    local_width = queries.shape[1]
    heads = local_width // HEAD_DIM
    rows = queries.shape[0]
    total_width = float(local_width * lax.axis_size("head"))
    q_wide = queries.astype(jnp.float32)
    dq_wide = query_tangent.astype(jnp.float32)
    k_wide = keys.astype(jnp.float32)
    dk_wide = key_tangent.astype(jnp.float32)
    sums = lax.psum(
        (
            jnp.sum(q_wide * q_wide, axis=1),
            jnp.sum(q_wide * dq_wide, axis=1),
            jnp.sum(k_wide * k_wide, axis=1),
            jnp.sum(k_wide * dk_wide, axis=1),
        ),
        "head",
    )
    normed_q, normed_dq = finish(q_wide, dq_wide, sums[0], sums[1], total_width, query_gain)
    normed_k, normed_dk = finish(k_wide, dk_wide, sums[2], sums[3], total_width, key_gain)
    q_heads = by_heads(normed_q, heads)
    dq_heads = by_heads(normed_dq, heads)
    initial = (
        jnp.full((heads, rows), -1e30, jnp.float32),
        jnp.zeros((heads, rows), jnp.float32),
        jnp.zeros((heads, rows), jnp.float32),
        jnp.zeros((heads, rows, HEAD_DIM), jnp.float32),
        jnp.zeros((heads, rows, HEAD_DIM), jnp.float32),
    )
    gathered = (
        lax.all_gather(normed_k, "ctx", axis=0, tiled=True),
        lax.all_gather(normed_dk, "ctx", axis=0, tiled=True),
        lax.all_gather(values, "ctx", axis=0, tiled=True),
        lax.all_gather(value_tangent, "ctx", axis=0, tiled=True),
    )
    piece_heads = tuple((by_heads(p, heads) for p in gathered))
    state = lax.map(head_update, (q_heads, dq_heads) + piece_heads + tuple(initial))
    running, total, spread, primal_sum, tangent_sum = state
    primal = primal_sum / total[:, :, None]
    tangent_out = tangent_sum / total[:, :, None] - (spread / total)[:, :, None] * primal
    attended = primal.transpose(1, 0, 2).reshape(rows, local_width).astype(jnp.bfloat16)
    attended_tangent = (
        tangent_out.transpose(1, 0, 2).reshape(rows, local_width).astype(jnp.bfloat16)
    )
    return (attended, attended_tangent)


def solution(mesh):
    placed = (
        P(("dp", "ctx"), "head"),
        P(("dp", "ctx"), "head"),
        P(("dp", "ctx"), "head"),
        P(("dp", "ctx"), "head"),
        P(("dp", "ctx"), "head"),
        P(("dp", "ctx"), "head"),
        P("head"),
        P("head"),
    )
    return jax.shard_map(
        shards,
        mesh=mesh,
        in_specs=placed,
        out_specs=(P(("dp", "ctx"), "head"), P(("dp", "ctx"), "head")),
        check_vma=False,
    )
```

profile of v0, /device:TPU:16, one launch (start us, length us, event | category | flops | bytes accessed | tf_op | source)
XLA Modules:
  0.0 531.7 jit_solution(12822888990173604877)
XLA Ops:
  7.2 1.7 copy.12
  10.5 21.5 %all-reduce = (f32[768]{0:T(1024)S(1)}, f32[128]{0:T(128)S(1)}, f32[768]{0:T(1024)S(1)}, f32[128]{0:T(128)S(1)}) all-reduce(f32[768]{0:T(1024)S(1)} %get-tuple-element.80, f32[128]{0:T(128)S(1)} %get-tuple-element.82, f32[768]{0:T(1024)S(1)} %get-tuple-element.79, ...), channel_id=1, replica_groups=mesh['ctx'=16,'head'=8,'dp'=2] {'head'}, use_global_device_ids=true, to_apply=%region_1.0 | all-reduce | flops 1792 | bytes 14336 | tf_op jit(solution)/shard_map/psum | solution.py:72
  35.5 1.9 fusion.47
  37.5 84.9 %all-gather.5.cloned.1.call-done = bf16[2048,640]{0,1:T(8,128)(2,1)} async-done(((bf16[128,640]{0,1:T(8,128)(2,1)}), bf16[2048,640]{0,1:T(8,128)(2,1)}) %all-gather.5.cloned.1.call-update) | async-done | bytes 2621456 | tf_op jit(solution)/shard_map/all_gather | solution.py:93
  122.3 92.5 %all-gather.7.cloned.1.call-done = bf16[2048,640]{0,1:T(8,128)(2,1)} async-done(((bf16[128,640]{0,1:T(8,128)(2,1)}), bf16[2048,640]{0,1:T(8,128)(2,1)}) %all-gather.7.cloned.1.call-update) | async-done | bytes 2621456 | tf_op jit(solution)/shard_map/all_gather | solution.py:94
  214.9 92.5 %all-gather.9.cloned.1.call-done = bf16[2048,640]{0,1:T(8,128)(2,1)} async-done(((bf16[128,640]{0,1:T(8,128)(2,1)}), bf16[2048,640]{0,1:T(8,128)(2,1)}) %all-gather.9.cloned.1.call-update) | async-done | bytes 2621456 | tf_op jit(solution)/shard_map/all_gather | solution.py:95
  307.4 92.4 %all-gather.11.cloned.1.call-done = bf16[2048,640]{0,1:T(8,128)(2,1)} async-done(((bf16[128,640]{0,1:T(8,128)(2,1)}), bf16[2048,640]{0,1:T(8,128)(2,1)}) %all-gather.11.cloned.1.call-update) | async-done | bytes 2621456 | tf_op jit(solution)/shard_map/all_gather | solution.py:96
  399.8 119.4 %while.16 = (s32[]{:T(128)}, f32[5,768]{1,0:T(8,128)}, f32[5,768]{1,0:T(8,128)}, f32[5,768,128]{1,2,0:T(8,128)}, f32[5,768,128]{1,2,0:T(8,128)}, /*index=5*/bf16...) while((s32[]{:T(128)}, f32[5,768]{1,0:T(8,128)}, ...), condition=%wide.region_12.13_spmd, body=%wide.region_8.12_spmd.sunk | while | flops 2444527872 | bytes 84033696 | solution.py:99
  399.8 2.2 multiply_reduce_fusion.2
  402.0 2.8 fusion.86
  404.8 3.5 fusion.87
  408.3 1.2 fusion.88
  409.4 2.4 fusion.91
  411.8 0.9 copy.45
  412.7 4.0 fusion.89
  416.7 2.1 fusion.90
  419.0 1.9 constant_dynamic-update-slice_fusion.3
  420.9 1.3 dynamic_update_slice.21
  422.3 1.4 dynamic_update_slice.20
  423.6 2.2 multiply_reduce_fusion.2
  425.9 2.8 fusion.86
  428.6 3.5 fusion.87
  432.1 1.2 fusion.88
  433.3 2.4 fusion.91
  435.7 0.9 copy.45
  436.6 4.0 fusion.89
  440.6 2.1 fusion.90
  442.8 2.0 constant_dynamic-update-slice_fusion.3
  444.8 1.3 dynamic_update_slice.21
  446.2 1.4 dynamic_update_slice.20
  447.5 2.2 multiply_reduce_fusion.2
  449.8 2.8 fusion.86
  452.5 3.5 fusion.87
  456.0 1.2 fusion.88
  457.2 2.4 fusion.91
  459.6 0.9 copy.45
  460.5 4.0 fusion.89
  464.5 2.1 fusion.90
  466.7 1.9 constant_dynamic-update-slice_fusion.3
  468.7 1.3 dynamic_update_slice.21
  470.0 1.4 dynamic_update_slice.20
  471.4 2.2 multiply_reduce_fusion.2
  473.6 2.8 fusion.86
  476.4 3.5 fusion.87
  479.9 1.2 fusion.88
  481.1 2.4 fusion.91
  484.4 4.0 fusion.89
  488.4 2.1 fusion.90
  490.6 2.0 constant_dynamic-update-slice_fusion.3
  492.6 1.3 dynamic_update_slice.21
  493.9 1.4 dynamic_update_slice.20
  495.3 2.2 multiply_reduce_fusion.2
  497.5 2.8 fusion.86
  500.3 3.5 fusion.87
  503.8 1.2 fusion.88
  505.0 2.4 fusion.91
  508.2 4.0 fusion.89
  512.2 2.1 fusion.90
  514.5 1.9 constant_dynamic-update-slice_fusion.3
  516.4 1.3 dynamic_update_slice.21
  517.8 1.4 dynamic_update_slice.20
  519.9 2.6 subtract_convert_fusion
  522.5 1.3 copy.26
  523.8 1.3 copy.27
  (74 shorter events, 8.5 us)
Async XLA Ops:
  7.2 1.8 copy-start.1
  7.2 2.4 copy-start.2
  7.2 2.6 copy-start.3
  7.2 115.1 %all-gather.5.cloned.1.call-start = ((), (), s32[]{:S(2)}) async-start(), calls=%async_computation | async-start | bytes 2785280 | tf_op jit(solution)/shard_map/all_gather | solution.py:93
  8.9 23.1 %copy-start.6 = (f32[640]{0:T(1024)S(1)}, f32[640]{0:T(1024)}, u32[]{:S(2)}) copy-start(f32[640]{0:T(1024)} %param.17) | copy-start | bytes 7684
  8.9 24.8 %copy-start.4 = (bf16[128,640]{1,0:T(8,128)(2,1)S(1)}, bf16[128,640]{1,0:T(8,128)(2,1)}, u32[]{:S(2)}) copy-start(bf16[128,640]{1,0:T(8,128)(2,1)} %param.14) | copy-start | bytes 491524
  9.6 25.0 %copy-start.5 = (bf16[128,640]{1,0:T(8,128)(2,1)S(1)}, bf16[128,640]{1,0:T(8,128)(2,1)}, u32[]{:S(2)}) copy-start(bf16[128,640]{1,0:T(8,128)(2,1)} %param.15) | copy-start | bytes 491524
  9.6 25.9 %copy-start.7 = (f32[640]{0:T(1024)S(1)}, f32[640]{0:T(1024)}, u32[]{:S(2)}) copy-start(f32[640]{0:T(1024)} %param.16) | copy-start | bytes 7684
  33.0 181.9 %all-gather.7.cloned.1.call-start = ((), (), s32[]{:S(2)}) async-start(), calls=%async_computation.1 | async-start | bytes 2785280 | tf_op jit(solution)/shard_map/all_gather | solution.py:94
  33.7 273.7 %all-gather.9.cloned.1.call-start = ((), (), s32[]{:S(2)}) async-start(), calls=%async_computation.2 | async-start | bytes 2785280 | tf_op jit(solution)/shard_map/all_gather | solution.py:95
  34.6 365.2 %all-gather.11.cloned.1.call-start = ((), (), s32[]{:S(2)}) async-start(), calls=%async_computation.3 | async-start | bytes 2785280 | tf_op jit(solution)/shard_map/all_gather | solution.py:96
  402.0 7.4 %copy-start = (f32[768,2048]{1,0:T(8,128)}, f32[768,2048]{1,0:T(8,128)S(1)}, u32[]{:S(2)}) copy-start(f32[768,2048]{1,0:T(8,128)S(1)} %get-tuple-element.209) | copy-start | bytes 18874372 | tf_op jit(solution)/shard_map/while
  425.8 7.5 %copy-start = (f32[768,2048]{1,0:T(8,128)}, f32[768,2048]{1,0:T(8,128)S(1)}, u32[]{:S(2)}) copy-start(f32[768,2048]{1,0:T(8,128)S(1)} %get-tuple-element.209) | copy-start | bytes 18874372 | tf_op jit(solution)/shard_map/while
  449.7 7.4 %copy-start = (f32[768,2048]{1,0:T(8,128)}, f32[768,2048]{1,0:T(8,128)S(1)}, u32[]{:S(2)}) copy-start(f32[768,2048]{1,0:T(8,128)S(1)} %get-tuple-element.209) | copy-start | bytes 18874372 | tf_op jit(solution)/shard_map/while
  473.6 7.4 %copy-start = (f32[768,2048]{1,0:T(8,128)}, f32[768,2048]{1,0:T(8,128)S(1)}, u32[]{:S(2)}) copy-start(f32[768,2048]{1,0:T(8,128)S(1)} %get-tuple-element.209) | copy-start | bytes 18874372 | tf_op jit(solution)/shard_map/while
  497.5 7.4 %copy-start = (f32[768,2048]{1,0:T(8,128)}, f32[768,2048]{1,0:T(8,128)S(1)}, u32[]{:S(2)}) copy-start(f32[768,2048]{1,0:T(8,128)S(1)} %get-tuple-element.209) | copy-start | bytes 18874372 | tf_op jit(solution)/shard_map/while
Sparse Core Ops, SparseCore 0:
  33.1 89.2 all-gather.4
  124.0 90.7 all-gather.6
  216.6 90.7 all-gather.8
  309.0 90.7 all-gather.10
where the time goes:
time: 539 us; the launch traced here: 532 us
  waiting for transfers between devices  363 us (67%)
  matrix products  84.5 us (16%)
  local copies, waits for them, and re-layouts  35.7 us (7%)
  blocking collectives  21.5 us (4%)
  between operations  14 us (3%)
  other arithmetic  12.5 us (2%)
    all_gather x1, waiting for transfers between devices, shards(): lax.all_gather(values, 'ctx', axis=0, tiled=True)  92.5 us
    all_gather x1, waiting for transfers between devices, shards(): lax.all_gather(normed_dk, 'ctx', axis=0, tiled=True)  92.5 us
    all_gather x1, waiting for transfers between devices, shards(): lax.all_gather(value_tangent, 'ctx', axis=0, tiled=True)  92.4 us
    all_gather x1, waiting for transfers between devices, shards(): lax.all_gather(normed_k, 'ctx', axis=0, tiled=True)  84.9 us
    dynamic_update_slice x25, local copies, waits for them, and re-layouts, shards(): lax.map(head_update, (q_heads, dq_heads) + piece_heads + tuple(initial))  28.7 us
    psum x1, blocking collectives, shards(): lax.psum((jnp.sum(q_wide * q_wide, axis=1), jnp.sum(q_wide * dq_wide, axi...  21.5 us
    dot_general x5, matrix products, head_update(): jnp.dot(weights_low, dv_head, preferred_element_type=jnp.float32)  20 us
    dot_general x5, matrix products, head_update(): jnp.einsum('qd,kd->qk', q_head, dk_head, preferred_element_type=jnp.float32)  17.3 us
  transfers between devices with their start and end apart: 4, of which 4 were waited for; matrix products, arithmetic and copies ran while one was open for 1% of the time, Pallas kernels for 0%

commit v1 on v0

v1 whole, which is shorter than its diff:
```python
import functools

import jax
import jax.numpy as jnp
from jax import lax
from jax.experimental import pallas as pl
from jax.experimental.pallas import tpu as pltpu
from jax.sharding import PartitionSpec as P

HEAD_DIM = 128
MESH = pl.DeviceIdType.MESH
ROWS = 768
BLOCK = 128
QT = 256
EPS = 1e-6
LOG2E = 1.4426950408889634
F32 = jnp.float32
BF16 = jnp.bfloat16


def kernel(
    width,
    n_head,
    n_z,
    q_hbm,
    dq_hbm,
    k_hbm,
    dk_hbm,
    v_hbm,
    dv_hbm,
    qg_ref,
    kg_ref,
    oa_hbm,
    ot_hbm,
    q_in,
    dq_in,
    k_in,
    dk_in,
    stat,
    coef,
    qq,
    q_send,
    kv,
    k_send,
    acc,
    m_ref,
    l_ref,
    sp_ref,
    out,
    in_sem,
    vl_sem,
    st_s,
    st_r,
    yv_s,
    yv_r,
    yk_s,
    yk_r,
    yq_s,
    yq_r,
    z_s,
    z_r,
    o_s,
    o_r,
):
    c = lax.axis_index("ctx")
    h = lax.axis_index("head")
    p = lax.axis_index("dp")
    z = lax.div(c, 2)
    y = lax.rem(c, 2)
    other = 2 * z + 1 - y
    right = (2 * lax.rem(z + 1, n_z) + y, h, p)
    left = (2 * lax.rem(z + n_z - 1, n_z) + y, h, p)
    across = (other, h, p)
    head_peers = [(c, lax.rem(h + i, n_head), p) for i in range(1, n_head)]
    scale = HEAD_DIM ** (-0.5)
    n_q = ROWS // QT
    q_blocks = ROWS // BLOCK

    barrier = pltpu.get_barrier_semaphore()
    for peer in [right, left, across] + head_peers:
        pl.semaphore_signal(barrier, inc=1, device_id=peer, device_id_type=MESH)

    def mine(x):
        return pl.multiple_of((2 * y + x if x < 2 else 4) * HEAD_DIM, HEAD_DIM)

    def theirs(x):
        return pl.multiple_of((2 * (1 - y) + x if x < 2 else 4) * HEAD_DIM, HEAD_DIM)

    loads = [
        pltpu.make_async_copy(src, dst, in_sem.at[i])
        for i, (src, dst) in enumerate(
            ((k_hbm, k_in), (dk_hbm, dk_in), (q_hbm, q_in), (dq_hbm, dq_in))
        )
    ]
    for load in loads:
        load.start()
    v_loads = [
        pltpu.make_async_copy(
            src.at[:, pl.ds(mine(x), HEAD_DIM)],
            kv.at[x, 0, c, :, pl.ds(half * HEAD_DIM, HEAD_DIM)],
            vl_sem.at[x, half],
        )
        for x in range(3)
        for half, src in enumerate((v_hbm, dv_hbm))
    ]
    for load in v_loads:
        load.start()

    def row_sums(a, b):
        field = a.astype(F32)
        tangent = b.astype(F32)
        square = field * field
        cross = field * tangent
        folded = [
            functools.reduce(
                jnp.add, [t[:, i : i + BLOCK] for i in range(0, width, BLOCK)]
            )
            for t in (square, cross)
        ]
        return [jnp.sum(t.T, axis=0, keepdims=True) for t in folded]

    loads[0].wait()
    loads[1].wait()
    sums_k = row_sums(k_in[...], dk_in[...])
    stat[h, 6:7, :] = sums_k[0]
    stat[h, 7:8, :] = jnp.zeros((1, BLOCK), F32)
    stat[h, 14:15, :] = sums_k[1]
    stat[h, 15:16, :] = jnp.zeros((1, BLOCK), F32)
    loads[2].wait()
    loads[3].wait()
    for r in range(q_blocks):
        rows = slice(r * BLOCK, (r + 1) * BLOCK)
        sums_q = row_sums(q_in[rows, :], dq_in[rows, :])
        stat[h, r : r + 1, :] = sums_q[0]
        stat[h, 8 + r : 9 + r, :] = sums_q[1]

    pl.semaphore_wait(barrier, 3 + len(head_peers))

    stat_sends = [
        pltpu.make_async_remote_copy(
            stat.at[h],
            stat.at[h],
            st_s.at[i],
            st_r.at[h],
            device_id=peer,
            device_id_type=MESH,
        )
        for i, peer in enumerate(head_peers)
    ]
    for send in stat_sends:
        send.start()

    yv_sends = [
        pltpu.make_async_remote_copy(
            src.at[:, pl.ds(theirs(x), HEAD_DIM)],
            kv.at[x, 0, c, :, pl.ds(half * HEAD_DIM, HEAD_DIM)],
            yv_s.at[x, half],
            yv_r.at[x, half],
            device_id=across,
            device_id_type=MESH,
        )
        for x in range(3)
        for half, src in enumerate((v_hbm, dv_hbm))
    ]
    for send in yv_sends:
        send.start()

    def ring(x, part, slot, direction, typ, hop):
        return pltpu.make_async_remote_copy(
            kv.at[x, part, slot],
            kv.at[x, part, slot],
            z_s.at[direction, x, part, typ, hop],
            z_r.at[x, part, slot],
            device_id=right if direction == 0 else left,
            device_id_type=MESH,
        )

    def first_hop(x, part, typ):
        slot = c if typ == 0 else other
        for direction in range(2):
            ring(x, part, slot, direction, typ, 0).start()

    for load in v_loads:
        load.wait()
    for x in range(3):
        first_hop(x, 0, 0)

    for i in range(1, n_head):
        sender = lax.rem(h + i, n_head)
        pltpu.make_async_remote_copy(
            stat.at[sender],
            stat.at[sender],
            st_s.at[i - 1],
            st_r.at[sender],
            device_id=head_peers[i - 1],
            device_id_type=MESH,
        ).wait_recv()
    total = functools.reduce(jnp.add, [stat[i] for i in range(n_head)])
    mean = total * (1.0 / (width * n_head))
    inverse = lax.rsqrt(mean[:8] + EPS)
    coef[0:8, :] = inverse
    coef[8:16, :] = inverse * inverse * inverse * mean[8:]

    def normed(field, tangent, gain, inv, third):
        field = field.astype(F32)
        tangent = tangent.astype(F32)
        return (
            (field * inv * gain).astype(BF16),
            (gain * (tangent * inv - field * third)).astype(BF16),
        )

    def spread_rows(row):
        return jnp.broadcast_to(coef[row : row + 1, :], (BLOCK, BLOCK)).T

    inv_k, third_k = spread_rows(6), spread_rows(14)

    def norm_keys(columns, store):
        cols = pl.ds(columns, HEAD_DIM)
        n, dn = normed(k_in[:, cols], dk_in[:, cols], kg_ref[:, cols], inv_k, third_k)
        store[:, 0:HEAD_DIM] = n
        store[:, HEAD_DIM:] = dn

    yk_sends = []
    for x in range(3):
        norm_keys(mine(x), kv.at[x, 1, c])
        if x < 2:
            norm_keys(theirs(x), k_send.at[x])
        send = pltpu.make_async_remote_copy(
            k_send.at[x] if x < 2 else kv.at[x, 1, c],
            kv.at[x, 1, c],
            yk_s.at[x],
            yk_r.at[x],
            device_id=across,
            device_id_type=MESH,
        )
        send.start()
        yk_sends.append(send)
        first_hop(x, 1, 0)

    def arrived_across(x, part):
        if part == 1:
            pltpu.make_async_remote_copy(
                kv.at[x, 1, other],
                kv.at[x, 1, other],
                yk_s.at[x],
                yk_r.at[x],
                device_id=across,
                device_id_type=MESH,
            ).wait_recv()
        else:
            for half, src in enumerate((v_hbm, dv_hbm)):
                pltpu.make_async_remote_copy(
                    src.at[:, pl.ds(theirs(x), HEAD_DIM)],
                    kv.at[x, 0, other, :, pl.ds(half * HEAD_DIM, HEAD_DIM)],
                    yv_s.at[x, half],
                    yv_r.at[x, half],
                    device_id=across,
                    device_id_type=MESH,
                ).wait_recv()

    for x in range(3):
        arrived_across(x, 0)
        first_hop(x, 0, 1)

    def norm_queries(columns, store):
        cols = pl.ds(columns, HEAD_DIM)
        gain = qg_ref[:, cols]
        for r in range(q_blocks):
            rows = slice(r * BLOCK, (r + 1) * BLOCK)
            n, dn = normed(
                q_in[rows, cols], dq_in[rows, cols], gain, spread_rows(r), spread_rows(8 + r)
            )
            store[rows, 0:HEAD_DIM] = dn
            store[rows, HEAD_DIM:] = n

    def q_across(x, i):
        return pltpu.make_async_remote_copy(
            q_send.at[x, pl.ds(i * QT, QT)],
            qq.at[x, pl.ds(ROWS + i * QT, QT)],
            yq_s.at[x, i],
            yq_r.at[x, i],
            device_id=across,
            device_id_type=MESH,
        )

    norm_queries(theirs(0), q_send.at[0])
    for i in range(n_q):
        q_across(0, i).start()
    for x in range(3):
        arrived_across(x, 1)
        first_hop(x, 1, 1)
    norm_queries(theirs(1), q_send.at[1])
    for i in range(n_q):
        q_across(1, i).start()
    for x in range(3):
        norm_queries(mine(x), qq.at[x, pl.ds(0, ROWS)])

    def slot_of(zz, typ):
        return 2 * zz + jnp.where(typ == 0, y, 1 - y)

    last = n_z // 2

    def arrive(x, d, part, typ):
        from_left = slot_of(lax.rem(z + n_z - d, n_z), typ)
        from_right = slot_of(lax.rem(z + d, n_z), typ)

        @pl.when(jnp.logical_or(d < last, typ == 0))
        def _():
            ring(x, part, from_left, 0, typ, 0).wait_recv()

        @pl.when(jnp.logical_or(d < last - 1, jnp.logical_and(d == last - 1, typ == 0)))
        def _():
            ring(x, part, from_left, 0, typ, d).start()

        @pl.when(jnp.logical_or(d < last, typ == 1))
        def _():
            ring(x, part, from_right, 1, typ, 0).wait_recv()

        @pl.when(jnp.logical_or(d < last - 1, jnp.logical_and(d == last - 1, typ == 1)))
        def _():
            ring(x, part, from_right, 1, typ, d).start()

    def own_copy(x, i, which):
        cols = pl.ds(pl.multiple_of(jnp.where(x < 2, 2 * y + x, 4) * HEAD_DIM, HEAD_DIM), HEAD_DIM)
        rows = pl.ds(pl.multiple_of(i * QT, QT), QT)
        return pltpu.make_async_copy(
            out.at[which, x, rows],
            (oa_hbm, ot_hbm)[which].at[rows, cols],
            o_s.at[which, x, i],
        )

    def copy_across(x, i, which):
        cols = pl.ds(pl.multiple_of((2 * y + x) * HEAD_DIM, HEAD_DIM), HEAD_DIM)
        return pltpu.make_async_remote_copy(
            out.at[which, x, pl.ds(pl.multiple_of(ROWS + i * QT, QT), QT)],
            (oa_hbm, ot_hbm)[which].at[pl.ds(pl.multiple_of(i * QT, QT), QT), cols],
            o_s.at[which, x, n_q + i],
            o_r.at[which, x, i],
            device_id=across,
            device_id_type=MESH,
        )

    def tile(x, d, t):
        rows = pl.ds(pl.multiple_of(t * QT, QT), QT)
        far = lax.rem(z + d, n_z)
        near = lax.rem(z + n_z - lax.rem(d, last), n_z)

        @pl.when(jnp.logical_and(d == 1, t >= n_q))
        def _():
            q_across(x, t - n_q).wait_recv()

        @pl.when(d == 1)
        def _():
            acc[rows, :] = jnp.zeros((QT, 2 * HEAD_DIM), F32)
            m_ref[rows, :] = jnp.full((QT, HEAD_DIM), -1e30, F32)
            l_ref[rows, :] = jnp.zeros((QT, HEAD_DIM), F32)
            sp_ref[rows, :] = jnp.zeros((QT, HEAD_DIM), F32)

        pair = qq[x, rows, :]
        query = pair[:, HEAD_DIM:]
        contract = (((1,), (1,)), ((), ()))
        scores, tangents, vals = [], [], []
        for zz in (far, near):
            keys = kv[x, 1, pl.ds(2 * zz, 2)].reshape(2 * BLOCK, 2 * HEAD_DIM)
            vals.append(kv[x, 0, pl.ds(2 * zz, 2)].reshape(2 * BLOCK, 2 * HEAD_DIM))
            scores.append(
                lax.dot_general(
                    query, keys[:, :HEAD_DIM], contract, preferred_element_type=F32
                )
            )
            tangents.append(
                lax.dot_general(pair, keys, contract, preferred_element_type=F32)
            )
        top = jnp.max(jnp.maximum(scores[0], scores[1]), axis=1, keepdims=True)
        before = m_ref[rows, :]
        newest = jnp.maximum(before, top * (scale * LOG2E))
        factor = jnp.exp2(before - newest)
        shift = newest[:, 0:1]
        m_ref[rows, :] = newest
        total_w = l_ref[rows, :] * factor
        total_m = sp_ref[rows, :] * factor
        primal = acc[rows, 0:HEAD_DIM] * factor
        tangent = acc[rows, HEAD_DIM:] * factor
        for s, st, v in zip(scores, tangents, vals):
            w = jnp.exp2(s * (scale * LOG2E) - shift)
            mix = w * st
            for i in range(0, 2 * BLOCK, HEAD_DIM):
                total_w = total_w + w[:, i : i + HEAD_DIM]
                total_m = total_m + mix[:, i : i + HEAD_DIM]
            both = jnp.dot(w.astype(BF16), v, preferred_element_type=F32)
            mixed = jnp.dot(mix.astype(BF16), v[:, :HEAD_DIM], preferred_element_type=F32)
            primal = primal + both[:, :HEAD_DIM]
            tangent = tangent + both[:, HEAD_DIM:] + mixed * scale
        l_ref[rows, :] = total_w
        sp_ref[rows, :] = total_m
        acc[rows, 0:HEAD_DIM] = primal
        acc[rows, HEAD_DIM:] = tangent

        @pl.when(d == last)
        def _():
            whole = jnp.sum(l_ref[rows, :], axis=1, keepdims=True)
            inv = 1.0 / whole
            ratio = jnp.sum(sp_ref[rows, :], axis=1, keepdims=True) * scale * inv
            first = acc[rows, 0:HEAD_DIM] * inv
            out[0, x, rows, :] = first.astype(BF16)
            out[1, x, rows, :] = (acc[rows, HEAD_DIM:] * inv - ratio * first).astype(BF16)

            @pl.when(t < n_q)
            def _():
                for which in range(2):
                    own_copy(x, t, which).start()

            @pl.when(t >= n_q)
            def _():
                for which in range(2):
                    copy_across(x, t - n_q, which).start()

    steps = 3 * last

    def step(g, carry):
        x, d = lax.div(g, last), lax.rem(g, last) + 1
        before = jnp.maximum(g - 1, 0)
        xb, db = lax.div(before, last), lax.rem(before, last) + 1
        tiles = jnp.where(g == 0, 0, jnp.where(xb == 2, n_q, 2 * n_q))

        def sub(i, carry):
            @pl.when(g < steps)
            def _():
                arrive(x, d, lax.div(i, 2), lax.rem(i, 2))

            lax.fori_loop(
                lax.div(tiles * i, 4),
                lax.div(tiles * (i + 1), 4),
                lambda t, carry: (tile(xb, db, t), carry)[1],
                0,
            )
            return carry

        lax.fori_loop(0, 4, sub, 0)
        return carry

    lax.fori_loop(0, steps + 1, step, 0)

    for send in stat_sends + yv_sends + yk_sends:
        send.wait_send()
    for x in range(2):
        for i in range(n_q):
            q_across(x, i).wait_send()

    def drain(i, carry):
        x, part = lax.div(i, 2), lax.rem(i, 2)
        for typ in range(2):
            for hop in range(last):
                for direction in range(2):
                    if hop < last - 1 or direction == typ:
                        ring(x, part, c, direction, typ, hop).wait_send()
        return carry

    lax.fori_loop(0, 6, drain, 0)

    def drain_out(i, carry):
        for which in range(2):
            for x in range(3):
                own_copy(x, i, which).wait()
                if x < 2:
                    copy_across(x, i, which).wait_send()
                    copy_across(x, i, which).wait_recv()
        return carry

    lax.fori_loop(0, n_q, drain_out, 0)


def shards(mesh, queries, query_tangent, keys, key_tangent, values, value_tangent, query_gain, key_gain):
    n_head = mesh.shape["head"]
    n_z = mesh.shape["ctx"] // 2
    width = queries.shape[1]
    dma = pltpu.SemaphoreType.DMA
    anywhere = pl.BlockSpec(memory_space=pl.ANY)
    vmem = pl.BlockSpec(memory_space=pltpu.VMEM)
    n_q = ROWS // QT
    return tuple(pl.pallas_call(
        functools.partial(kernel, width, n_head, n_z),
        out_shape=[jax.ShapeDtypeStruct(queries.shape, BF16)] * 2,
        in_specs=[anywhere] * 6 + [vmem] * 2,
        out_specs=[anywhere] * 2,
        scratch_shapes=[
            pltpu.VMEM((ROWS, width), BF16),
            pltpu.VMEM((ROWS, width), BF16),
            pltpu.VMEM((BLOCK, width), BF16),
            pltpu.VMEM((BLOCK, width), BF16),
            pltpu.VMEM((n_head, 16, BLOCK), F32),
            pltpu.VMEM((16, BLOCK), F32),
            pltpu.VMEM((3, 2 * ROWS, 2 * HEAD_DIM), BF16),
            pltpu.VMEM((2, ROWS, 2 * HEAD_DIM), BF16),
            pltpu.VMEM((3, 2, 2 * n_z, BLOCK, 2 * HEAD_DIM), BF16),
            pltpu.VMEM((2, BLOCK, 2 * HEAD_DIM), BF16),
            pltpu.VMEM((2 * ROWS, 2 * HEAD_DIM), F32),
            pltpu.VMEM((2 * ROWS, HEAD_DIM), F32),
            pltpu.VMEM((2 * ROWS, HEAD_DIM), F32),
            pltpu.VMEM((2 * ROWS, HEAD_DIM), F32),
            pltpu.VMEM((2, 3, 2 * ROWS, HEAD_DIM), BF16),
            dma((4,)),
            dma((3, 2)),
            dma((n_head - 1,)),
            dma((n_head,)),
            dma((3, 2)),
            dma((3, 2)),
            dma((3,)),
            dma((3,)),
            dma((2, n_q)),
            dma((2, n_q)),
            dma((2, 3, 2, 2, n_z // 2)),
            dma((3, 2, 2 * n_z)),
            dma((2, 3, 2 * n_q)),
            dma((2, 2, n_q)),
        ],
        compiler_params=pltpu.CompilerParams(
            collective_id=0, has_side_effects=True, vmem_limit_bytes=62 * 2**20
        ),
        cost_estimate=pl.CostEstimate(
            flops=12 * 5 * ROWS * 16 * BLOCK * HEAD_DIM,
            bytes_accessed=5 * 2**20,
            transcendentals=5 * ROWS * 16 * BLOCK,
        ),
    )(
        queries,
        query_tangent,
        keys,
        key_tangent,
        values,
        value_tangent,
        query_gain.reshape(1, width),
        key_gain.reshape(1, width),
    ))


def solution(mesh):
    rows = P(("dp", "ctx"), "head")
    return jax.shard_map(
        functools.partial(shards, mesh),
        mesh=mesh,
        in_specs=(rows,) * 6 + (P("head"),) * 2,
        out_specs=(rows, rows),
        check_vma=False,
    )
```

time: 539 us -> 99 us (0.18); the launches traced: 532 us -> 97.6 us
  waiting for transfers between devices: 363 us -> 0 us
  Pallas kernels: 0 us -> 91.8 us
  matrix products: 84.5 us -> 0 us
  local copies, waits for them, and re-layouts: 35.7 us -> 5.12 us
  blocking collectives: 21.5 us -> 0 us
  between operations: 14 us -> 0.66 us
  other arithmetic: 12.5 us -> 0 us
    all_gather x4 -> x0, waiting for transfers between devices: 362 us -> none  [the longest x1 92.5 us: shards(): lax.all_gather(values, 'ctx', axis=0, tiled=True)]
    pallas_call x0 -> x1, Pallas kernels: none -> 91.8 us  [shards(): pl.pallas_call(functools.partial(kernel, width, n_head, n_z), out_shape=[...]
    dot_general x30 -> x0, matrix products: 84.5 us -> none  [the longest x5 20 us: head_update(): jnp.dot(weights_low, dv_head, preferred_element_type=jnp.float32)]
    dynamic_update_slice x25 -> x0, local copies, waits for them, and re-layouts: 28.7 us -> none  [shards(): lax.map(head_update, (q_heads, dq_heads) + piece_heads + tuple(initial))]
    psum x1 -> x0, blocking collectives: 21.5 us -> none  [shards(): lax.psum((jnp.sum(q_wide * q_wide, axis=1), jnp.sum(q_wide * dq_wide, axi...]
    reduce_sum x7 -> x0, other arithmetic: 6.29 us -> none  [the longest x5 5.78 us: head_update(): total = factor * total + jnp.sum(weights, axis=1)]
    convert_element_type x3 -> x0, other arithmetic: 5.4 us -> none  [the longest x2 2.82 us: finish(): (gain * (tangent * inverse - field * inverse ** 3 * mean_cross)).astype(j...]
  transfers between devices with their start and end apart: 4 -> 0, of which waited for: 4 -> 0; matrix products, arithmetic and copies ran while one was open for 1% -> 0% of each run, Pallas kernels for 0% -> 0%
where the time goes in v1:
time: 99 us; the launch traced here: 97.6 us
  Pallas kernels  91.8 us (93%)
  local copies, waits for them, and re-layouts  5.12 us (5%)
    pallas_call x1, Pallas kernels, shards(): pl.pallas_call(functools.partial(kernel, width, n_head, n_z), out_shape=[...  91.8 us
    unnamed x6, local copies, waits for them, and re-layouts  3.27 us

profile of v1, /device:TPU:16, one launch (start us, length us, event | category | flops | bytes accessed | tf_op | source)
XLA Modules:
  0.0 97.6 jit_solution(267538467420600020)
XLA Ops:
  0.6 0.0 copy-start.1
  0.6 1.3 %reshape.10.qg_ref = f32[1,640]{1,0:T(1,128)} reshape(f32[640]{0:T(1024)} %param.14) | data formatting | bytes 5120 | tf_op jit(solution)/shard_map/reshape | solution.py:532
  1.9 0.0 copy-done.1
  1.9 0.6 reshape.11.kg_ref
  2.5 91.8 %shard_map.95 = (bf16[768,640]{1,0:T(8,128)(2,1)}, bf16[768,640]{1,0:T(8,128)(2,1)}) custom-call(bf16[768,640]{1,0:T(8,128)(2,1)} %q_hbm.1, bf16[768,640]{1,0:T(8,128)(2,1)} %dq_hbm.1, bf16[128,640]{1,0:T(8,128)(2,1)} %k_hbm.1, bf16[128,640]{1,0:T(8,128)(2,1)} %dk_hbm.1, bf16[128,640]{1,0:T(8,128)(2,1)} %v_hbm.1, bf16[128,640]{1,0:T(8,128)(2,1)} %dv_hbm.1, ...), custom_call_target="tpu_custom_call" | custom-call | flops 12079595520 | bytes 5242880 | tf_op jit(solution)/shard_map/pallas_call | solution.py:481
  94.3 0.0 copy-start
  94.3 2.3 %copy.12 = bf16[768,640]{1,0:T(8,128)(2,1)} copy(bf16[768,640]{1,0:T(8,128)(2,1)} %get-tuple-element.4) | data formatting | bytes 1966080
  96.6 0.0 copy-done
  96.6 0.9 copy.13
Async XLA Ops:
  0.6 1.3 %copy-start.1 = (f32[640]{0:T(1024)S(1)}, f32[640]{0:T(1024)}, u32[]{:S(2)}) copy-start(f32[640]{0:T(1024)} %param.15) | copy-start | bytes 7684
  94.3 2.3 %copy-start = (bf16[768,640]{1,0:T(8,128)(2,1)S(1)}, bf16[768,640]{1,0:T(8,128)(2,1)}, u32[]{:S(2)}) copy-start(bf16[768,640]{1,0:T(8,128)(2,1)} %get-tuple-element.5) | copy-start | bytes 2949124

commit v2 on v1

v2 whole, which is shorter than its diff:
```python
import functools

import jax
import jax.numpy as jnp
from jax import lax
from jax.experimental import pallas as pl
from jax.experimental.pallas import tpu as pltpu
from jax.sharding import PartitionSpec as P

HEAD_DIM = 128
MESH = pl.DeviceIdType.MESH
ROWS = 768
BLOCK = 128
QT = 768
EPS = 1e-6
ORDER = ((0, 1), (0, 2), (1, 1), (0, 3), (1, 2), (0, 4), (1, 3), (1, 4), (2, 1), (2, 2), (2, 3), (2, 4))
LOG2E = 1.4426950408889634
F32 = jnp.float32
BF16 = jnp.bfloat16


def by_pair(x, part, d):
    return False if isinstance(x, int) else x > 9


def kernel(
    width,
    n_head,
    n_z,
    q_hbm,
    dq_hbm,
    k_hbm,
    dk_hbm,
    v_hbm,
    dv_hbm,
    qg_ref,
    kg_ref,
    oa_hbm,
    ot_hbm,
    q_in,
    dq_in,
    k_in,
    dk_in,
    stat,
    coef,
    qq,
    q_send,
    kv,
    k_send,
    acc,
    m_ref,
    l_ref,
    sp_ref,
    out,
    in_sem,
    vl_sem,
    st_s,
    st_r,
    yv_s,
    yv_r,
    yk_s,
    yk_r,
    yq_s,
    yq_r,
    z_s,
    z_r,
    p_s,
    o_s,
    o_r,
):
    c = lax.axis_index("ctx")
    h = lax.axis_index("head")
    p = lax.axis_index("dp")
    z = lax.div(c, 2)
    y = lax.rem(c, 2)
    right = (2 * lax.rem(z + 1, n_z) + y, h, p)
    left = (2 * lax.rem(z + n_z - 1, n_z) + y, h, p)
    across = (2 * z + 1 - y, h, p)
    head_peers = [(c, lax.rem(h + i, n_head), p) for i in range(1, n_head)]
    scale = HEAD_DIM ** (-0.5)
    last = n_z // 2
    home = n_z - 1
    n_q = ROWS // QT
    q_blocks = ROWS // BLOCK

    barrier = pltpu.get_barrier_semaphore()
    for peer in [right, left, across] + head_peers:
        pl.semaphore_signal(barrier, inc=1, device_id=peer, device_id_type=MESH)

    def mine(x):
        return pl.multiple_of((2 * y + x if x < 2 else 4) * HEAD_DIM, HEAD_DIM)

    def theirs(x):
        return pl.multiple_of((2 * (1 - y) + x if x < 2 else 4) * HEAD_DIM, HEAD_DIM)

    v_loads = [
        pltpu.make_async_copy(
            src.at[:, pl.ds(mine(x), HEAD_DIM)],
            kv.at[x, 0, home, 0, :, pl.ds(half * HEAD_DIM, HEAD_DIM)],
            vl_sem.at[x, half],
        )
        for x in range(3)
        for half, src in enumerate((v_hbm, dv_hbm))
    ]
    for load in v_loads:
        load.start()

    loads = [
        pltpu.make_async_copy(src, dst, in_sem.at[i])
        for i, (src, dst) in enumerate(
            ((k_hbm, k_in), (dk_hbm, dk_in), (q_hbm, q_in), (dq_hbm, dq_in))
        )
    ]
    for load in loads:
        load.start()
    pl.semaphore_wait(barrier, 3 + len(head_peers))

    yv_sends = [
        pltpu.make_async_remote_copy(
            src.at[:, pl.ds(theirs(x), HEAD_DIM)],
            kv.at[x, 0, home, 1, :, pl.ds(half * HEAD_DIM, HEAD_DIM)],
            yv_s.at[x, half],
            yv_r.at[x, half],
            device_id=across,
            device_id_type=MESH,
        )
        for x in range(3)
        for half, src in enumerate((v_hbm, dv_hbm))
    ]
    for send in yv_sends:
        send.start()

    def ring(x, part, typ, direction, hop):
        src = jnp.where(hop == 0, home, 2 * (hop - 1) + direction)
        dst = jnp.minimum(2 * hop + direction, home - 1)
        return pltpu.make_async_remote_copy(
            kv.at[x, part, src, typ],
            kv.at[x, part, dst, typ],
            z_s.at[direction, x, part, typ, hop],
            z_r.at[x, part, dst, typ],
            device_id=right if direction == 0 else left,
            device_id_type=MESH,
        )

    def first_hop(x, part, typ):
        for direction in range(2):
            ring(x, part, typ, direction, 0).start()

    for x in range(3):
        v_loads[2 * x].wait()
        v_loads[2 * x + 1].wait()
        first_hop(x, 0, 0)

    def row_sums(a, b):
        field = a.astype(F32)
        tangent = b.astype(F32)
        square = field * field
        cross = field * tangent
        folded = [
            functools.reduce(
                jnp.add, [t[:, i : i + BLOCK] for i in range(0, width, BLOCK)]
            )
            for t in (square, cross)
        ]
        return [jnp.sum(t.T, axis=0, keepdims=True) for t in folded]

    loads[0].wait()
    loads[1].wait()
    sums_k = row_sums(k_in[...], dk_in[...])
    stat[h, 6:7, :] = sums_k[0]
    stat[h, 7:8, :] = jnp.zeros((1, BLOCK), F32)
    stat[h, 14:15, :] = sums_k[1]
    stat[h, 15:16, :] = jnp.zeros((1, BLOCK), F32)
    loads[2].wait()
    loads[3].wait()
    for r in range(q_blocks):
        rows = slice(r * BLOCK, (r + 1) * BLOCK)
        sums_q = row_sums(q_in[rows, :], dq_in[rows, :])
        stat[h, r : r + 1, :] = sums_q[0]
        stat[h, 8 + r : 9 + r, :] = sums_q[1]

    stat_sends = [
        pltpu.make_async_remote_copy(
            stat.at[h],
            stat.at[h],
            st_s.at[i],
            st_r.at[h],
            device_id=peer,
            device_id_type=MESH,
        )
        for i, peer in enumerate(head_peers)
    ]
    for send in stat_sends:
        send.start()

    def arrived_across(x, part):
        if part == 1:
            pltpu.make_async_remote_copy(
                kv.at[x, 1, home, 0],
                kv.at[x, 1, home, 1],
                yk_s.at[x],
                yk_r.at[x],
                device_id=across,
                device_id_type=MESH,
            ).wait_recv()
        else:
            for half, src in enumerate((v_hbm, dv_hbm)):
                pltpu.make_async_remote_copy(
                    src.at[:, pl.ds(theirs(x), HEAD_DIM)],
                    kv.at[x, 0, home, 1, :, pl.ds(half * HEAD_DIM, HEAD_DIM)],
                    yv_s.at[x, half],
                    yv_r.at[x, half],
                    device_id=across,
                    device_id_type=MESH,
                ).wait_recv()

    for x in range(3):
        arrived_across(x, 0)
        if not by_pair(x, 0, 1):
            first_hop(x, 0, 1)

    for i in range(1, n_head):
        sender = lax.rem(h + i, n_head)
        pltpu.make_async_remote_copy(
            stat.at[sender],
            stat.at[sender],
            st_s.at[i - 1],
            st_r.at[sender],
            device_id=head_peers[i - 1],
            device_id_type=MESH,
        ).wait_recv()
    total = functools.reduce(jnp.add, [stat[i] for i in range(n_head)])
    mean = total * (1.0 / (width * n_head))
    inverse = lax.rsqrt(mean[:8] + EPS)
    coef[0:8, :] = inverse
    coef[8:16, :] = inverse * inverse * inverse * mean[8:]

    def normed(field, tangent, gain, inv, third):
        field = field.astype(F32)
        tangent = tangent.astype(F32)
        return (
            (field * inv * gain).astype(BF16),
            (gain * (tangent * inv - field * third)).astype(BF16),
        )

    def spread_rows(row):
        return jnp.broadcast_to(coef[row : row + 1, :], (BLOCK, BLOCK)).T

    inv_k, third_k = spread_rows(6), spread_rows(14)

    def norm_keys(columns, store):
        cols = pl.ds(columns, HEAD_DIM)
        n, dn = normed(k_in[:, cols], dk_in[:, cols], kg_ref[cols].reshape(1, HEAD_DIM), inv_k, third_k)
        store[:, 0:HEAD_DIM] = n
        store[:, HEAD_DIM:] = dn

    yk_sends = []
    for x in range(3):
        norm_keys(mine(x), kv.at[x, 1, home, 0])
        if x < 2:
            norm_keys(theirs(x), k_send.at[x])
        send = pltpu.make_async_remote_copy(
            k_send.at[x] if x < 2 else kv.at[x, 1, home, 0],
            kv.at[x, 1, home, 1],
            yk_s.at[x],
            yk_r.at[x],
            device_id=across,
            device_id_type=MESH,
        )
        send.start()
        yk_sends.append(send)
        first_hop(x, 1, 0)

    def norm_queries(columns, store):
        cols = pl.ds(columns, HEAD_DIM)
        gain = qg_ref[cols].reshape(1, HEAD_DIM)
        for r in range(q_blocks):
            rows = slice(r * BLOCK, (r + 1) * BLOCK)
            n, dn = normed(
                q_in[rows, cols], dq_in[rows, cols], gain, spread_rows(r), spread_rows(8 + r)
            )
            store[rows, 0:HEAD_DIM] = dn
            store[rows, HEAD_DIM:] = n

    def q_across(x, i):
        return pltpu.make_async_remote_copy(
            q_send.at[x, pl.ds(i * QT, QT)],
            qq.at[x, pl.ds(ROWS + i * QT, QT)],
            yq_s.at[x, i],
            yq_r.at[x, i],
            device_id=across,
            device_id_type=MESH,
        )

    norm_queries(theirs(0), q_send.at[0])
    for i in range(n_q):
        q_across(0, i).start()
    for x in range(3):
        arrived_across(x, 1)
        if not by_pair(x, 1, 1):
            first_hop(x, 1, 1)
    norm_queries(theirs(1), q_send.at[1])
    for i in range(n_q):
        q_across(1, i).start()
    for x in range(3):
        norm_queries(mine(x), qq.at[x, pl.ds(0, ROWS)])

    def over(x, part, d, direction):
        pos = jnp.minimum(2 * (d - 1) + direction, home - 1)
        return pltpu.make_async_remote_copy(
            kv.at[x, part, pos, 0],
            kv.at[x, part, pos, 1],
            p_s.at[x, part, pos],
            z_r.at[x, part, pos, 1],
            device_id=across,
            device_id_type=MESH,
        )

    def arrive(x, d, part, typ):
        paired = by_pair(x, part, d)
        paired_next = by_pair(x, part, d + 1)
        for direction in range(2):
            here = jnp.logical_or(d < last, typ == direction)
            on = jnp.logical_or(d < last - 1, jnp.logical_and(d == last - 1, typ == direction))

            from_pair = jnp.logical_and(paired, typ == 1)
            by_ring = jnp.logical_and(here, jnp.logical_not(from_pair))
            by_other = jnp.logical_and(
                from_pair, jnp.logical_or(d < last, direction == 0)
            )

            @pl.when(by_ring)
            def _():
                ring(x, part, typ, direction, d - 1).wait_recv()

            @pl.when(by_other)
            def _():
                over(x, part, d, direction).wait_recv()

            @pl.when(jnp.logical_and(on, jnp.logical_not(jnp.logical_and(paired_next, typ == 1))))
            def _():
                ring(x, part, typ, direction, d).start()

            @pl.when(jnp.logical_and(jnp.logical_and(paired, typ == 0), here))
            def _():
                over(x, part, d, direction).start()

    def own_copy(x, i, which):
        cols = pl.ds(pl.multiple_of(jnp.where(x < 2, 2 * y + x, 4) * HEAD_DIM, HEAD_DIM), HEAD_DIM)
        rows = pl.ds(pl.multiple_of(i * QT, QT), QT)
        return pltpu.make_async_copy(
            out.at[which, x, rows],
            (oa_hbm, ot_hbm)[which].at[rows, cols],
            o_s.at[which, x, i],
        )

    def copy_across(x, i, which):
        cols = pl.ds(pl.multiple_of((2 * y + x) * HEAD_DIM, HEAD_DIM), HEAD_DIM)
        return pltpu.make_async_remote_copy(
            out.at[which, x, pl.ds(pl.multiple_of(ROWS + i * QT, QT), QT)],
            (oa_hbm, ot_hbm)[which].at[pl.ds(pl.multiple_of(i * QT, QT), QT), cols],
            o_s.at[which, x, n_q + i],
            o_r.at[which, x, i],
            device_id=across,
            device_id_type=MESH,
        )

    def tile(x, d, t):
        rows = pl.ds(pl.multiple_of(t * QT, QT), QT)
        @pl.when(jnp.logical_and(d == 1, t >= n_q))
        def _():
            q_across(x, t - n_q).wait_recv()

        @pl.when(d == 1)
        def _():
            acc[x, rows, :] = jnp.zeros((QT, 2 * HEAD_DIM), F32)
            m_ref[x, rows, :] = jnp.full((QT, HEAD_DIM), -1e30, F32)
            l_ref[x, rows, :] = jnp.zeros((QT, HEAD_DIM), F32)
            sp_ref[x, rows, :] = jnp.zeros((QT, HEAD_DIM), F32)

        pair = qq[x, rows, :]
        query = pair[:, HEAD_DIM:]
        contract = (((1,), (1,)), ((), ()))
        keys = kv[x, 1, pl.ds(2 * (d - 1), 2)].reshape(4 * BLOCK, 2 * HEAD_DIM)
        vals = kv[x, 0, pl.ds(2 * (d - 1), 2)].reshape(4 * BLOCK, 2 * HEAD_DIM)
        scores = lax.dot_general(query, keys[:, :HEAD_DIM], contract, preferred_element_type=F32)
        slopes = lax.dot_general(pair, keys, contract, preferred_element_type=F32)
        top = jnp.max(scores, axis=1, keepdims=True)
        before = m_ref[x, rows, :]
        newest = jnp.maximum(before, top * (scale * LOG2E))
        factor = jnp.exp2(before - newest)
        m_ref[x, rows, :] = newest
        total_w = l_ref[x, rows, :] * factor
        total_m = sp_ref[x, rows, :] * factor
        w = jnp.exp2(scores * (scale * LOG2E) - newest[:, 0:1])
        mix = w * slopes
        for i in range(0, 4 * BLOCK, HEAD_DIM):
            total_w = total_w + w[:, i : i + HEAD_DIM]
            total_m = total_m + mix[:, i : i + HEAD_DIM]
        both = jnp.dot(w.astype(BF16), vals, preferred_element_type=F32)
        mixed = jnp.dot(mix.astype(BF16), vals[:, :HEAD_DIM], preferred_element_type=F32)
        primal = acc[x, rows, 0:HEAD_DIM] * factor + both[:, :HEAD_DIM]
        tangent = acc[x, rows, HEAD_DIM:] * factor + both[:, HEAD_DIM:] + mixed * scale
        l_ref[x, rows, :] = total_w
        sp_ref[x, rows, :] = total_m
        acc[x, rows, 0:HEAD_DIM] = primal
        acc[x, rows, HEAD_DIM:] = tangent

        @pl.when(d == last)
        def _():
            whole = jnp.sum(l_ref[x, rows, :], axis=1, keepdims=True)
            inv = 1.0 / whole
            ratio = jnp.sum(sp_ref[x, rows, :], axis=1, keepdims=True) * scale * inv
            first = acc[x, rows, 0:HEAD_DIM] * inv
            out[0, x, rows, :] = first.astype(BF16)
            out[1, x, rows, :] = (acc[x, rows, HEAD_DIM:] * inv - ratio * first).astype(BF16)

            @pl.when(t < n_q)
            def _():
                for which in range(2):
                    own_copy(x, t, which).start()

            @pl.when(t >= n_q)
            def _():
                for which in range(2):
                    copy_across(x, t - n_q, which).start()

    steps = 3 * last

    def turn(g):
        order = ORDER
        x, d = order[-1]
        for i, (xi, di) in enumerate(order[:-1]):
            x = jnp.where(g == i, xi, x)
            d = jnp.where(g == i, di, d)
        return x, d

    def step(g, carry):
        x, d = turn(g)
        xb, db = turn(jnp.maximum(g - 1, 0))
        tiles = jnp.where(g == 0, 0, jnp.where(xb == 2, n_q, 2 * n_q))

        def sub(i, carry):
            @pl.when(g < steps)
            def _():
                arrive(x, d, lax.div(i, 2), lax.rem(i, 2))

            lax.fori_loop(
                lax.div(tiles * i, 4),
                lax.div(tiles * (i + 1), 4),
                lambda t, carry: (
                    tile(xb, db, jnp.where(db == last, tiles - 1 - t, t)),
                    carry,
                )[1],
                0,
            )
            return carry

        lax.fori_loop(0, 4, sub, 0)
        return carry

    lax.fori_loop(0, steps + 1, step, 0)

    for send in stat_sends + yv_sends + yk_sends:
        send.wait_send()
    for x in range(2):
        for i in range(n_q):
            q_across(x, i).wait_send()

    def drain(i, carry):
        x, part = lax.div(i, 2), lax.rem(i, 2)
        for typ in range(2):
            for hop in range(last):
                for direction in range(2):
                    if hop < last - 1 or direction == typ:

                        @pl.when(jnp.logical_not(jnp.logical_and(by_pair(x, part, hop + 1), typ == 1)))
                        def _():
                            ring(x, part, typ, direction, hop).wait_send()

                    if typ == 0 and (hop < last - 1 or direction == 0):

                        @pl.when(by_pair(x, part, hop + 1))
                        def _():
                            over(x, part, hop + 1, direction).wait_send()

        return carry

    lax.fori_loop(0, 6, drain, 0)

    def drain_out(i, carry):
        for which in range(2):
            for x in range(3):
                own_copy(x, i, which).wait()
                if x < 2:
                    copy_across(x, i, which).wait_send()
                    copy_across(x, i, which).wait_recv()
        return carry

    lax.fori_loop(0, n_q, drain_out, 0)


def copies(oa_src, ot_src, oa_dst, ot_dst, held, load_sem, store_sem):
    parts = 2
    size = ROWS // parts
    loads, stores = [], []
    for i in range(parts):
        rows = pl.ds(i * size, size)
        for j, (src, dst) in enumerate(((oa_src, oa_dst), (ot_src, ot_dst))):
            loads.append(pltpu.make_async_copy(src.at[rows], held.at[j, rows], load_sem.at[j, i]))
            stores.append(pltpu.make_async_copy(held.at[j, rows], dst.at[rows], store_sem.at[j, i]))
    for load in loads:
        load.start()
    for load, store in zip(loads, stores):
        load.wait()
        store.start()
    for store in stores:
        store.wait()


def settle(first, second):
    anywhere = pl.BlockSpec(memory_space=pl.ANY)
    return tuple(
        pl.pallas_call(
            copies,
            out_shape=[jax.ShapeDtypeStruct(first.shape, BF16)] * 2,
            in_specs=[anywhere] * 2,
            out_specs=[anywhere] * 2,
            scratch_shapes=[
                pltpu.VMEM((2,) + first.shape, BF16),
                pltpu.SemaphoreType.DMA((2, 2)),
                pltpu.SemaphoreType.DMA((2, 2)),
            ],
            compiler_params=pltpu.CompilerParams(vmem_limit_bytes=62 * 2**20),
        )(first, second)
    )


def shards(mesh, queries, query_tangent, keys, key_tangent, values, value_tangent, query_gain, key_gain):
    n_head = mesh.shape["head"]
    n_z = mesh.shape["ctx"] // 2
    width = queries.shape[1]
    dma = pltpu.SemaphoreType.DMA
    anywhere = pl.BlockSpec(memory_space=pl.ANY)
    vmem = pl.BlockSpec(memory_space=pltpu.VMEM)
    n_q = ROWS // QT
    results = pl.pallas_call(
        functools.partial(kernel, width, n_head, n_z),
        out_shape=[jax.ShapeDtypeStruct(queries.shape, BF16)] * 2,
        in_specs=[anywhere] * 6 + [vmem] * 2,
        out_specs=[anywhere] * 2,
        scratch_shapes=[
            pltpu.VMEM((ROWS, width), BF16),
            pltpu.VMEM((ROWS, width), BF16),
            pltpu.VMEM((BLOCK, width), BF16),
            pltpu.VMEM((BLOCK, width), BF16),
            pltpu.VMEM((n_head, 16, BLOCK), F32),
            pltpu.VMEM((16, BLOCK), F32),
            pltpu.VMEM((3, 2 * ROWS, 2 * HEAD_DIM), BF16),
            pltpu.VMEM((2, ROWS, 2 * HEAD_DIM), BF16),
            pltpu.VMEM((3, 2, n_z, 2, BLOCK, 2 * HEAD_DIM), BF16),
            pltpu.VMEM((2, BLOCK, 2 * HEAD_DIM), BF16),
            pltpu.VMEM((3, 2 * ROWS, 2 * HEAD_DIM), F32),
            pltpu.VMEM((3, 2 * ROWS, HEAD_DIM), F32),
            pltpu.VMEM((3, 2 * ROWS, HEAD_DIM), F32),
            pltpu.VMEM((3, 2 * ROWS, HEAD_DIM), F32),
            pltpu.VMEM((2, 3, 2 * ROWS, HEAD_DIM), BF16),
            dma((4,)),
            dma((3, 2)),
            dma((n_head - 1,)),
            dma((n_head,)),
            dma((3, 2)),
            dma((3, 2)),
            dma((3,)),
            dma((3,)),
            dma((2, n_q)),
            dma((2, n_q)),
            dma((2, 3, 2, 2, n_z // 2)),
            dma((3, 2, n_z, 2)),
            dma((3, 2, n_z)),
            dma((2, 3, 2 * n_q)),
            dma((2, 2, n_q)),
        ],
        compiler_params=pltpu.CompilerParams(
            collective_id=0, has_side_effects=True, vmem_limit_bytes=62 * 2**20
        ),
        cost_estimate=pl.CostEstimate(
            flops=12 * 5 * ROWS * 16 * BLOCK * HEAD_DIM,
            bytes_accessed=5 * 2**20,
            transcendentals=5 * ROWS * 16 * BLOCK,
        ),
    )(
        queries,
        query_tangent,
        keys,
        key_tangent,
        values,
        value_tangent,
        query_gain,
        key_gain,
    )
    return settle(*results)


def solution(mesh):
    rows = P(("dp", "ctx"), "head")
    return jax.shard_map(
        functools.partial(shards, mesh),
        mesh=mesh,
        in_specs=(rows,) * 6 + (P("head"),) * 2,
        out_specs=(rows, rows),
        check_vma=False,
    )
```

time: 99 us -> 86.3 us (0.87)
  Pallas kernels: 91.8 us -> 84.3 us
  local copies, waits for them, and re-layouts: 5.12 us -> 0 us
    pallas_call x1, Pallas kernels: 91.8 us -> 82 us  [shards(): pl.pallas_call(functools.partial(kernel, width, n_head, n_z), out_shape=[...]
    unnamed x6 -> x0, local copies, waits for them, and re-layouts: 3.27 us -> none
    pallas_call x0 -> x1, Pallas kernels: none -> 2.36 us  [settle(): pl.pallas_call(copies, out_shape=[jax.ShapeDtypeStruct(first.shape, BF16)...]
    reshape x2 -> x0, local copies, waits for them, and re-layouts: 1.85 us -> none  [the longest x1 1.27 us: shards(): query_gain.reshape(1, width)]
where the time goes in v2:
time: 86.3 us; the launch traced here: 85 us
  Pallas kernels  84.3 us (98%)
    pallas_call x1, Pallas kernels, shards(): pl.pallas_call(functools.partial(kernel, width, n_head, n_z), out_shape=[...  82 us
    pallas_call x1, Pallas kernels, settle(): pl.pallas_call(copies, out_shape=[jax.ShapeDtypeStruct(first.shape, BF16)...  2.36 us

profile of v2, /device:TPU:16, one launch (start us, length us, event | category | flops | bytes accessed | tf_op | source)
XLA Modules:
  0.0 85.0 jit_solution(5981181157919200999)
XLA Ops:
  0.6 82.0 %shard_map.95 = (bf16[768,640]{1,0:T(8,128)(2,1)}, bf16[768,640]{1,0:T(8,128)(2,1)}) custom-call(bf16[768,640]{1,0:T(8,128)(2,1)} %q_hbm.1, bf16[768,640]{1,0:T(8,128)(2,1)} %dq_hbm.1, bf16[128,640]{1,0:T(8,128)(2,1)} %k_hbm.1, bf16[128,640]{1,0:T(8,128)(2,1)} %dk_hbm.1, bf16[128,640]{1,0:T(8,128)(2,1)} %v_hbm.1, bf16[128,640]{1,0:T(8,128)(2,1)} %dv_hbm.1, ...), custom_call_target="tpu_custom_call" | custom-call | flops 12079595520 | bytes 5242880 | tf_op jit(solution)/shard_map/pallas_call | solution.py:547
  82.6 2.4 %shard_map.96 = (bf16[768,640]{1,0:T(8,128)(2,1)}, bf16[768,640]{1,0:T(8,128)(2,1)}) custom-call(bf16[768,640]{1,0:T(8,128)(2,1)} %get-tuple-element.4.oa_src, bf16[768,640]{1,0:T(8,128)(2,1)} %get-tuple-element.5.ot_src), custom_call_target="tpu_custom_call" | custom-call | tf_op jit(solution)/shard_map/pallas_call | solution.py:524

commit v3 on v2

--- a/solution.py
+++ b/solution.py
@@ -13,14 +13,11 @@
 BLOCK = 128
 QT = 768
 EPS = 1e-6
-ORDER = ((0, 1), (0, 2), (1, 1), (0, 3), (1, 2), (0, 4), (1, 3), (1, 4), (2, 1), (2, 2), (2, 3), (2, 4))
+ORDER = ((0, 1), (0, 2), (1, 1), (0, 3), (1, 2), (0, 4), (1, 3), (2, 1), (1, 4), (2, 2), (2, 3), (2, 4))
+SECOND_STARTS, THIRD_STARTS = 0, 5
 LOG2E = 1.4426950408889634
 F32 = jnp.float32
 BF16 = jnp.bfloat16
-
-
-def by_pair(x, part, d):
-    return False if isinstance(x, int) else x > 9
 
 
 def kernel(
@@ -64,7 +61,6 @@
     yq_r,
     z_s,
     z_r,
-    p_s,
     o_s,
     o_r,
 ):
@@ -127,7 +123,7 @@
         for x in range(3)
         for half, src in enumerate((v_hbm, dv_hbm))
     ]
-    for send in yv_sends:
+    for send in yv_sends[:4]:
         send.start()
 
     def ring(x, part, typ, direction, hop):
@@ -214,10 +210,8 @@
                     device_id_type=MESH,
                 ).wait_recv()
 
-    for x in range(3):
-        arrived_across(x, 0)
-        if not by_pair(x, 0, 1):
-            first_hop(x, 0, 1)
+    arrived_across(0, 0)
+    first_hop(0, 0, 1)
 
     for i in range(1, n_head):
         sender = lax.rem(h + i, n_head)
@@ -254,12 +248,8 @@
         store[:, 0:HEAD_DIM] = n
         store[:, HEAD_DIM:] = dn
 
-    yk_sends = []
-    for x in range(3):
-        norm_keys(mine(x), kv.at[x, 1, home, 0])
-        if x < 2:
-            norm_keys(theirs(x), k_send.at[x])
-        send = pltpu.make_async_remote_copy(
+    yk_sends = [
+        pltpu.make_async_remote_copy(
             k_send.at[x] if x < 2 else kv.at[x, 1, home, 0],
             kv.at[x, 1, home, 1],
             yk_s.at[x],
@@ -267,9 +257,15 @@
             device_id=across,
             device_id_type=MESH,
         )
-        send.start()
-        yk_sends.append(send)
-        first_hop(x, 1, 0)
+        for x in range(3)
+    ]
+    for x in range(2):
+        norm_keys(theirs(x), k_send.at[x])
+        yk_sends[x].start()
+        norm_keys(mine(x), kv.at[x, 1, home, 0])
+        if x == 0:
+            first_hop(0, 1, 0)
+    norm_keys(mine(2), kv.at[2, 1, home, 0])
 
     def norm_queries(columns, store):
         cols = pl.ds(columns, HEAD_DIM)
@@ -295,55 +291,22 @@
     norm_queries(theirs(0), q_send.at[0])
     for i in range(n_q):
         q_across(0, i).start()
-    for x in range(3):
-        arrived_across(x, 1)
-        if not by_pair(x, 1, 1):
-            first_hop(x, 1, 1)
+    arrived_across(0, 1)
+    first_hop(0, 1, 1)
     norm_queries(theirs(1), q_send.at[1])
-    for i in range(n_q):
-        q_across(1, i).start()
     for x in range(3):
         norm_queries(mine(x), qq.at[x, pl.ds(0, ROWS)])
 
-    def over(x, part, d, direction):
-        pos = jnp.minimum(2 * (d - 1) + direction, home - 1)
-        return pltpu.make_async_remote_copy(
-            kv.at[x, part, pos, 0],
-            kv.at[x, part, pos, 1],
-            p_s.at[x, part, pos],
-            z_r.at[x, part, pos, 1],
-            device_id=across,
-            device_id_type=MESH,
-        )
-
     def arrive(x, d, part, typ):
-        paired = by_pair(x, part, d)
-        paired_next = by_pair(x, part, d + 1)
         for direction in range(2):
-            here = jnp.logical_or(d < last, typ == direction)
-            on = jnp.logical_or(d < last - 1, jnp.logical_and(d == last - 1, typ == direction))
-
-            from_pair = jnp.logical_and(paired, typ == 1)
-            by_ring = jnp.logical_and(here, jnp.logical_not(from_pair))
-            by_other = jnp.logical_and(
-                from_pair, jnp.logical_or(d < last, direction == 0)
-            )
-
-            @pl.when(by_ring)
+
+            @pl.when(jnp.logical_or(d < last, typ == direction))
             def _():
                 ring(x, part, typ, direction, d - 1).wait_recv()
 
-            @pl.when(by_other)
-            def _():
-                over(x, part, d, direction).wait_recv()
-
-            @pl.when(jnp.logical_and(on, jnp.logical_not(jnp.logical_and(paired_next, typ == 1))))
+            @pl.when(jnp.logical_or(d < last - 1, jnp.logical_and(d == last - 1, typ == direction)))
             def _():
                 ring(x, part, typ, direction, d).start()
-
-            @pl.when(jnp.logical_and(jnp.logical_and(paired, typ == 0), here))
-            def _():
-                over(x, part, d, direction).start()
 
     def own_copy(x, i, which):
         cols = pl.ds(pl.multiple_of(jnp.where(x < 2, 2 * y + x, 4) * HEAD_DIM, HEAD_DIM), HEAD_DIM)
@@ -440,20 +403,40 @@
         xb, db = turn(jnp.maximum(g - 1, 0))
         tiles = jnp.where(g == 0, 0, jnp.where(xb == 2, n_q, 2 * n_q))
 
+        @pl.when(g == 1)
+        def _():
+            for send in yv_sends[4:] + yk_sends[2:]:
+                send.start()
+
+        @pl.when(g == 2)
+        def _():
+            for i in range(n_q):
+                q_across(1, i).start()
+
         def sub(i, carry):
-            @pl.when(g < steps)
-            def _():
-                arrive(x, d, lax.div(i, 2), lax.rem(i, 2))
-
             lax.fori_loop(
-                lax.div(tiles * i, 4),
-                lax.div(tiles * (i + 1), 4),
+                lax.div(tiles * i + 3, 4),
+                lax.div(tiles * (i + 1) + 3, 4),
                 lambda t, carry: (
                     tile(xb, db, jnp.where(db == last, tiles - 1 - t, t)),
                     carry,
                 )[1],
                 0,
             )
+
+            @pl.when(g < steps)
+            def _():
+                arrive(x, d, lax.div(i, 2), lax.rem(i, 2))
+
+            for head, start in ((1, SECOND_STARTS), (2, THIRD_STARTS)):
+                for k, (part, typ) in enumerate(((0, 1), (1, 0), (1, 1))):
+
+                    @pl.when(jnp.logical_and(g == start, i == k))
+                    def _(head=head, part=part, typ=typ):
+                        if typ == 1:
+                            arrived_across(head, part)
+                        first_hop(head, part, typ)
+
             return carry
 
         lax.fori_loop(0, 4, sub, 0)
@@ -473,17 +456,7 @@
             for hop in range(last):
                 for direction in range(2):
                     if hop < last - 1 or direction == typ:
-
-                        @pl.when(jnp.logical_not(jnp.logical_and(by_pair(x, part, hop + 1), typ == 1)))
-                        def _():
-                            ring(x, part, typ, direction, hop).wait_send()
-
-                    if typ == 0 and (hop < last - 1 or direction == 0):
-
-                        @pl.when(by_pair(x, part, hop + 1))
-                        def _():
-                            over(x, part, hop + 1, direction).wait_send()
-
+                        ring(x, part, typ, direction, hop).wait_send()
         return carry
 
     lax.fori_loop(0, 6, drain, 0)
@@ -577,7 +550,6 @@
             dma((2, n_q)),
             dma((2, 3, 2, 2, n_z // 2)),
             dma((3, 2, n_z, 2)),
-            dma((3, 2, n_z)),
             dma((2, 3, 2 * n_q)),
             dma((2, 2, n_q)),
         ],

time: 86.3 us -> 80.9 us (0.937); the launches traced: 85 us -> 80.8 us
  Pallas kernels: 84.3 us -> 80.1 us
    pallas_call x1, Pallas kernels: 82 us -> 77.8 us  [shards(): pl.pallas_call(functools.partial(kernel, width, n_head, n_z), out_shape=[...]
where the time goes in v3:
time: 80.9 us; the launch traced here: 80.8 us
  Pallas kernels  80.1 us (99%)
    pallas_call x1, Pallas kernels, shards(): pl.pallas_call(functools.partial(kernel, width, n_head, n_z), out_shape=[...  77.8 us
    pallas_call x1, Pallas kernels, settle(): pl.pallas_call(copies, out_shape=[jax.ShapeDtypeStruct(first.shape, BF16)...  2.36 us

profile of v3, /device:TPU:16, one launch (start us, length us, event | category | flops | bytes accessed | tf_op | source)
XLA Modules:
  0.0 80.8 jit_solution(1098375432709333676)
XLA Ops:
  0.6 77.8 %shard_map.95 = (bf16[768,640]{1,0:T(8,128)(2,1)}, bf16[768,640]{1,0:T(8,128)(2,1)}) custom-call(bf16[768,640]{1,0:T(8,128)(2,1)} %q_hbm.1, bf16[768,640]{1,0:T(8,128)(2,1)} %dq_hbm.1, bf16[128,640]{1,0:T(8,128)(2,1)} %k_hbm.1, bf16[128,640]{1,0:T(8,128)(2,1)} %dk_hbm.1, bf16[128,640]{1,0:T(8,128)(2,1)} %v_hbm.1, bf16[128,640]{1,0:T(8,128)(2,1)} %dv_hbm.1, ...), custom_call_target="tpu_custom_call" | custom-call | flops 12079595520 | bytes 5242880 | tf_op jit(solution)/shard_map/pallas_call | solution.py:520
  78.4 2.4 %shard_map.96 = (bf16[768,640]{1,0:T(8,128)(2,1)}, bf16[768,640]{1,0:T(8,128)(2,1)}) custom-call(bf16[768,640]{1,0:T(8,128)(2,1)} %get-tuple-element.4.oa_src, bf16[768,640]{1,0:T(8,128)(2,1)} %get-tuple-element.5.ot_src), custom_call_target="tpu_custom_call" | custom-call | tf_op jit(solution)/shard_map/pallas_call | solution.py:497

commit v4 on v3

--- a/solution.py
+++ b/solution.py
@@ -79,10 +79,6 @@
     n_q = ROWS // QT
     q_blocks = ROWS // BLOCK
 
-    barrier = pltpu.get_barrier_semaphore()
-    for peer in [right, left, across] + head_peers:
-        pl.semaphore_signal(barrier, inc=1, device_id=peer, device_id_type=MESH)
-
     def mine(x):
         return pl.multiple_of((2 * y + x if x < 2 else 4) * HEAD_DIM, HEAD_DIM)
 
@@ -109,6 +105,10 @@
     ]
     for load in loads:
         load.start()
+    barrier = pltpu.get_barrier_semaphore()
+    for peer in [right, left, across] + head_peers:
+        pl.semaphore_signal(barrier, inc=1, device_id=peer, device_id_type=MESH)
+
     pl.semaphore_wait(barrier, 3 + len(head_peers))
 
     yv_sends = [
@@ -473,22 +473,15 @@
     lax.fori_loop(0, n_q, drain_out, 0)
 
 
-def copies(oa_src, ot_src, oa_dst, ot_dst, held, load_sem, store_sem):
-    parts = 2
-    size = ROWS // parts
-    loads, stores = [], []
-    for i in range(parts):
-        rows = pl.ds(i * size, size)
-        for j, (src, dst) in enumerate(((oa_src, oa_dst), (ot_src, ot_dst))):
-            loads.append(pltpu.make_async_copy(src.at[rows], held.at[j, rows], load_sem.at[j, i]))
-            stores.append(pltpu.make_async_copy(held.at[j, rows], dst.at[rows], store_sem.at[j, i]))
-    for load in loads:
-        load.start()
-    for load, store in zip(loads, stores):
-        load.wait()
-        store.start()
-    for store in stores:
-        store.wait()
+def copies(oa_src, ot_src, oa_dst, ot_dst, sem):
+    moves = [
+        pltpu.make_async_copy(src, dst, sem.at[j])
+        for j, (src, dst) in enumerate(((oa_src, oa_dst), (ot_src, ot_dst)))
+    ]
+    for move in moves:
+        move.start()
+    for move in moves:
+        move.wait()
 
 
 def settle(first, second):
@@ -499,12 +492,8 @@
             out_shape=[jax.ShapeDtypeStruct(first.shape, BF16)] * 2,
             in_specs=[anywhere] * 2,
             out_specs=[anywhere] * 2,
-            scratch_shapes=[
-                pltpu.VMEM((2,) + first.shape, BF16),
-                pltpu.SemaphoreType.DMA((2, 2)),
-                pltpu.SemaphoreType.DMA((2, 2)),
-            ],
-            compiler_params=pltpu.CompilerParams(vmem_limit_bytes=62 * 2**20),
+            scratch_shapes=[pltpu.SemaphoreType.DMA((2,))],
+            compiler_params=pltpu.CompilerParams(vmem_limit_bytes=4 * 2**20),
         )(first, second)
     )
 
@@ -519,7 +508,7 @@
     n_q = ROWS // QT
     results = pl.pallas_call(
         functools.partial(kernel, width, n_head, n_z),
-        out_shape=[jax.ShapeDtypeStruct(queries.shape, BF16)] * 2,
+        out_shape=[pltpu.VMEM(queries.shape, BF16)] * 2,
         in_specs=[anywhere] * 6 + [vmem] * 2,
         out_specs=[anywhere] * 2,
         scratch_shapes=[
@@ -554,7 +543,7 @@
             dma((2, 2, n_q)),
         ],
         compiler_params=pltpu.CompilerParams(
-            collective_id=0, has_side_effects=True, vmem_limit_bytes=62 * 2**20
+            collective_id=0, has_side_effects=True, vmem_limit_bytes=58 * 2**20
         ),
         cost_estimate=pl.CostEstimate(
             flops=12 * 5 * ROWS * 16 * BLOCK * HEAD_DIM,

time: 80.9 us -> 79.8 us (0.986)
  Pallas kernels: 80.1 us -> 79.1 us
    pallas_call x1, Pallas kernels: 2.36 us -> 1.29 us  [settle(): pl.pallas_call(copies, out_shape=[jax.ShapeDtypeStruct(first.shape, BF16)...]
where the time goes in v4:
time: 79.8 us; the launch traced here: 79.7 us
  Pallas kernels  79.1 us (99%)
    pallas_call x1, Pallas kernels, shards(): pl.pallas_call(functools.partial(kernel, width, n_head, n_z), out_shape=[...  77.8 us

profile of v4, /device:TPU:16, one launch (start us, length us, event | category | flops | bytes accessed | tf_op | source)
XLA Modules:
  0.0 79.7 jit_solution(7951957478418455658)
XLA Ops:
  0.6 77.8 %shard_map.95 = (bf16[768,640]{1,0:T(8,128)(2,1)S(1)}, bf16[768,640]{1,0:T(8,128)(2,1)S(1)}) custom-call(bf16[768,640]{1,0:T(8,128)(2,1)} %q_hbm.1, bf16[768,640]{1,0:T(8,128)(2,1)} %dq_hbm.1, bf16[128,640]{1,0:T(8,128)(2,1)} %k_hbm.1, bf16[128,640]{1,0:T(8,128)(2,1)} %dk_hbm.1, bf16[128,640]{1,0:T(8,128)(2,1)} %v_hbm.1, bf16[128,640]{1,0:T(8,128)(2,1)} %dv_hbm.1, ...), custom_call_target="tpu_custom_call" | custom-call | flops 12079595520 | bytes 5242880 | tf_op jit(solution)/shard_map/pallas_call | solution.py:509
  78.4 1.3 %shard_map.96 = (bf16[768,640]{1,0:T(8,128)(2,1)}, bf16[768,640]{1,0:T(8,128)(2,1)}) custom-call(bf16[768,640]{1,0:T(8,128)(2,1)S(1)} %get-tuple-element.4.oa_src, bf16[768,640]{1,0:T(8,128)(2,1)S(1)} %get-tuple-element.5.ot_src), custom_call_target="tpu_custom_call" | custom-call | tf_op jit(solution)/shard_map/pallas_call | solution.py:490

commit v5 on v4

--- a/solution.py
+++ b/solution.py
@@ -75,7 +75,7 @@
     head_peers = [(c, lax.rem(h + i, n_head), p) for i in range(1, n_head)]
     scale = HEAD_DIM ** (-0.5)
     last = n_z // 2
-    home = n_z - 1
+    home = 0
     n_q = ROWS // QT
     q_blocks = ROWS // BLOCK
 
@@ -127,8 +127,8 @@
         send.start()
 
     def ring(x, part, typ, direction, hop):
-        src = jnp.where(hop == 0, home, 2 * (hop - 1) + direction)
-        dst = jnp.minimum(2 * hop + direction, home - 1)
+        src = jnp.where(hop == 0, home, 2 * hop - 1 + direction)
+        dst = jnp.minimum(2 * hop + 1 + direction, n_z - 1)
         return pltpu.make_async_remote_copy(
             kv.at[x, part, src, typ],
             kv.at[x, part, dst, typ],
@@ -328,24 +328,13 @@
             device_id_type=MESH,
         )
 
-    def tile(x, d, t):
-        rows = pl.ds(pl.multiple_of(t * QT, QT), QT)
-        @pl.when(jnp.logical_and(d == 1, t >= n_q))
-        def _():
-            q_across(x, t - n_q).wait_recv()
-
-        @pl.when(d == 1)
-        def _():
-            acc[x, rows, :] = jnp.zeros((QT, 2 * HEAD_DIM), F32)
-            m_ref[x, rows, :] = jnp.full((QT, HEAD_DIM), -1e30, F32)
-            l_ref[x, rows, :] = jnp.zeros((QT, HEAD_DIM), F32)
-            sp_ref[x, rows, :] = jnp.zeros((QT, HEAD_DIM), F32)
-
+    def attend(x, rows, first, count):
         pair = qq[x, rows, :]
         query = pair[:, HEAD_DIM:]
         contract = (((1,), (1,)), ((), ()))
-        keys = kv[x, 1, pl.ds(2 * (d - 1), 2)].reshape(4 * BLOCK, 2 * HEAD_DIM)
-        vals = kv[x, 0, pl.ds(2 * (d - 1), 2)].reshape(4 * BLOCK, 2 * HEAD_DIM)
+        size = 2 * BLOCK * count
+        keys = kv[x, 1, pl.ds(first, count)].reshape(size, 2 * HEAD_DIM)
+        vals = kv[x, 0, pl.ds(first, count)].reshape(size, 2 * HEAD_DIM)
         scores = lax.dot_general(query, keys[:, :HEAD_DIM], contract, preferred_element_type=F32)
         slopes = lax.dot_general(pair, keys, contract, preferred_element_type=F32)
         top = jnp.max(scores, axis=1, keepdims=True)
@@ -357,7 +346,7 @@
         total_m = sp_ref[x, rows, :] * factor
         w = jnp.exp2(scores * (scale * LOG2E) - newest[:, 0:1])
         mix = w * slopes
-        for i in range(0, 4 * BLOCK, HEAD_DIM):
+        for i in range(0, size, HEAD_DIM):
             total_w = total_w + w[:, i : i + HEAD_DIM]
             total_m = total_m + mix[:, i : i + HEAD_DIM]
         both = jnp.dot(w.astype(BF16), vals, preferred_element_type=F32)
@@ -368,6 +357,23 @@
         sp_ref[x, rows, :] = total_m
         acc[x, rows, 0:HEAD_DIM] = primal
         acc[x, rows, HEAD_DIM:] = tangent
+
+    def tile(x, d, t):
+        rows = pl.ds(pl.multiple_of(t * QT, QT), QT)
+        @pl.when(jnp.logical_and(d == 1, t >= n_q))
+        def _():
+            q_across(x, t - n_q).wait_recv()
+
+        @pl.when(d == 1)
+        def _():
+            acc[x, rows, :] = jnp.zeros((QT, 2 * HEAD_DIM), F32)
+            m_ref[x, rows, :] = jnp.full((QT, HEAD_DIM), -1e30, F32)
+            l_ref[x, rows, :] = jnp.zeros((QT, HEAD_DIM), F32)
+            sp_ref[x, rows, :] = jnp.zeros((QT, HEAD_DIM), F32)
+
+        pl.when(d == 1)(lambda: attend(x, rows, 0, 3))
+        pl.when(jnp.logical_and(d > 1, d < last))(lambda: attend(x, rows, 2 * d - 1, 2))
+        pl.when(d == last)(lambda: attend(x, rows, n_z - 1, 1))
 
         @pl.when(d == last)
         def _():

time: 79.8 us -> 80 us (level)
  no operation moved by 1% of the time
where the time goes in v5:
time: 80 us; the launch traced here: 79.9 us
  Pallas kernels  79.3 us (99%)
    pallas_call x1, Pallas kernels, shards(): pl.pallas_call(functools.partial(kernel, width, n_head, n_z), out_shape=[...  78 us

profile of v5, /device:TPU:16, one launch (start us, length us, event | category | flops | bytes accessed | tf_op | source)
XLA Modules:
  0.0 79.9 jit_solution(4067760552846479462)
XLA Ops:
  0.6 78.0 %shard_map.95 = (bf16[768,640]{1,0:T(8,128)(2,1)S(1)}, bf16[768,640]{1,0:T(8,128)(2,1)S(1)}) custom-call(bf16[768,640]{1,0:T(8,128)(2,1)} %q_hbm.1, bf16[768,640]{1,0:T(8,128)(2,1)} %dq_hbm.1, bf16[128,640]{1,0:T(8,128)(2,1)} %k_hbm.1, bf16[128,640]{1,0:T(8,128)(2,1)} %dk_hbm.1, bf16[128,640]{1,0:T(8,128)(2,1)} %v_hbm.1, bf16[128,640]{1,0:T(8,128)(2,1)} %dv_hbm.1, ...), custom_call_target="tpu_custom_call" | custom-call | flops 12079595520 | bytes 5242880 | tf_op jit(solution)/shard_map/pallas_call | solution.py:515
  78.6 1.3 %shard_map.96 = (bf16[768,640]{1,0:T(8,128)(2,1)}, bf16[768,640]{1,0:T(8,128)(2,1)}) custom-call(bf16[768,640]{1,0:T(8,128)(2,1)S(1)} %get-tuple-element.4.oa_src, bf16[768,640]{1,0:T(8,128)(2,1)S(1)} %get-tuple-element.5.ot_src), custom_call_target="tpu_custom_call" | custom-call | tf_op jit(solution)/shard_map/pallas_call | solution.py:496

commit v6 on v4

--- a/solution.py
+++ b/solution.py
@@ -293,9 +293,7 @@
         q_across(0, i).start()
     arrived_across(0, 1)
     first_hop(0, 1, 1)
-    norm_queries(theirs(1), q_send.at[1])
-    for x in range(3):
-        norm_queries(mine(x), qq.at[x, pl.ds(0, ROWS)])
+    norm_queries(mine(0), qq.at[0, pl.ds(0, ROWS)])
 
     def arrive(x, d, part, typ):
         for direction in range(2):
@@ -410,8 +408,14 @@
 
         @pl.when(g == 2)
         def _():
+            norm_queries(theirs(1), q_send.at[1])
             for i in range(n_q):
                 q_across(1, i).start()
+            norm_queries(mine(1), qq.at[1, pl.ds(0, ROWS)])
+
+        @pl.when(g == 4)
+        def _():
+            norm_queries(mine(2), qq.at[2, pl.ds(0, ROWS)])
 
         def sub(i, carry):
             lax.fori_loop(

time: 79.8 us -> 79.7 us (level)
  no operation moved by 1% of the time
where the time goes in v6:
time: 79.7 us; the launch traced here: 79.5 us
  Pallas kernels  78.9 us (99%)
    pallas_call x1, Pallas kernels, shards(): pl.pallas_call(functools.partial(kernel, width, n_head, n_z), out_shape=[...  77.6 us

profile of v6, /device:TPU:16, one launch (start us, length us, event | category | flops | bytes accessed | tf_op | source)
XLA Modules:
  0.0 79.5 jit_solution(1668985174319374150)
XLA Ops:
  0.6 77.6 %shard_map.95 = (bf16[768,640]{1,0:T(8,128)(2,1)S(1)}, bf16[768,640]{1,0:T(8,128)(2,1)S(1)}) custom-call(bf16[768,640]{1,0:T(8,128)(2,1)} %q_hbm.1, bf16[768,640]{1,0:T(8,128)(2,1)} %dq_hbm.1, bf16[128,640]{1,0:T(8,128)(2,1)} %k_hbm.1, bf16[128,640]{1,0:T(8,128)(2,1)} %dk_hbm.1, bf16[128,640]{1,0:T(8,128)(2,1)} %v_hbm.1, bf16[128,640]{1,0:T(8,128)(2,1)} %dv_hbm.1, ...), custom_call_target="tpu_custom_call" | custom-call | flops 12079595520 | bytes 5242880 | tf_op jit(solution)/shard_map/pallas_call | solution.py:513
  78.2 1.3 %shard_map.96 = (bf16[768,640]{1,0:T(8,128)(2,1)}, bf16[768,640]{1,0:T(8,128)(2,1)}) custom-call(bf16[768,640]{1,0:T(8,128)(2,1)S(1)} %get-tuple-element.4.oa_src, bf16[768,640]{1,0:T(8,128)(2,1)S(1)} %get-tuple-element.5.ot_src), custom_call_target="tpu_custom_call" | custom-call | tf_op jit(solution)/shard_map/pallas_call | solution.py:494
